TPU v7x, 512 devices: a whole 4x4x16 slice. The times are simulated.
512 devices in a mesh: dom: 64 (over x, z), orb: 8 (over y, core).
Axes of the slice: x: 4, y: 4, z: 16, core: 2. Of those that a mesh axis runs over, the one named last changes fastest.
Arguments:
- orbitals: bfloat16 [3072, 64, 512], P('dom', 'orb'), may hold values from -6 to 6
- adjoint_source: bfloat16 [3072, 64, 512], P('dom', 'orb'), may hold values from -6 to 6
- eigenvalues: float32 [64], P('orb'), may hold values from -1 to -0.25
- cell_scale: float32 [3072], P('dom'), may hold values from 0.4 to 1.6
- base_potential: float32 [3072, 512], P('dom'), may hold values from 0.5 to 1.5
- stiffness: bfloat16 [512, 512], replicated, may hold values from -1.5 to 1.5, as said below
- face_perm: int32 [3072, 64], P('dom'), may hold values from 0 to 63, each once within a row
- restrict: bfloat16 [512, 64], replicated, may hold values from -0.25 to 0.25
- prolong: bfloat16 [64, 512], replicated, may hold values from -0.75 to 0.75
- owner: int32 [3072, 1], P('dom'), may hold values from 0 to 63; in each aligned block of 48 rows (0 to 47, 48 to 95, ...) at most 2 rows name the same one
- pot_slot: int32 [3072], P('dom'), may hold values from 0 to 63
- potential: float32 [4096, 64], P('dom'), may hold values from -6 to 6
Outputs:
- adjoint: bfloat16 [3072, 64, 512], P('dom', 'orb')
- updated: float32 [4096, 64], P('dom')
- applied: bfloat16 [3072, 64, 512], P('dom', 'orb')
Inputs may be any that keep to these rules, and one draw needn't show every extreme that they name: In the rows of one device no owner is named by more than 2 cells. `face_perm`: each row is a permutation. `stiffness`: symmetric.
All inputs are finite; a program needn't handle non-finite values.
Results may differ from a plain program's by a relative error of at most 0.0027.
Values sent between devices are 32-bit elements; how exact they have to be, the bound alone decides.
No kernel may reach another device: no remote copies, remote signals or barrier semaphores. Data moves between devices by JAX's collectives and lax.ppermute only.
A program may use at most 64 MiB of HBM per device.

v0:
```python
import jax
import jax.numpy as jnp
from jax import lax
from jax.sharding import PartitionSpec as P

ITERS = 4
relax = 0.25
step_rate = 0.1


def padded_2(block, sides, width):
    for axis, dim in sides:
        count = lax.axis_size(axis)
        forward = [(i, i + 1) for i in range(count - 1)]
        backward = [(target, source) for source, target in forward]
        low = lax.ppermute(
            lax.slice_in_dim(block, block.shape[dim] - width, None, axis=dim), axis, forward
        )
        high = lax.ppermute(lax.slice_in_dim(block, 0, width, axis=dim), axis, backward)
        block = jnp.concatenate([low, block, high], axis=dim)
    return block


def local(
    orbitals,
    adjoint_source,
    eigenvalues,
    cell_scale,
    base_potential,
    stiffness,
    face_perm,
    restrict,
    prolong,
    owner,
    pot_slot,
    potential,
):
    nodes = stiffness.shape[0]
    faces = face_perm.shape[1]
    pot_rows = potential.shape[0]
    n_domains = lax.axis_size("dom")
    cell_count = owner.shape[0]
    capacity = 2 * ((cell_count + n_domains - 1) // n_domains)
    onehot = (face_perm[:, :, None] == jnp.arange(faces, dtype=jnp.int32)[None, None, :]).astype(
        jnp.float32
    )

    def assemble_local(partial_sum):
        left_face = partial_sum[:, :, :faces]
        right_face = partial_sum[:, :, nodes - faces :]
        sent_right = jnp.einsum("ckj,cok->coj", onehot, right_face, precision=lax.Precision.HIGHEST)
        boundary = jnp.stack([left_face[0], sent_right[-1]], 0)
        padded = padded_2(boundary, (("dom", 0),), 1)
        left_next = jnp.concatenate([left_face[1:], padded[3][None]], 0)
        add_right = jnp.einsum("ckj,coj->cok", onehot, left_next, precision=lax.Precision.HIGHEST)
        add_left = jnp.concatenate([padded[0][None], sent_right[:-1]], 0)
        return jnp.concatenate(
            [
                left_face + add_left,
                partial_sum[:, :, faces : nodes - faces],
                right_face + add_right,
            ],
            2,
        )

    def operator(values_bf, values_full, shift):
        kinetic = jnp.dot(
            values_bf.reshape(-1, nodes), stiffness, preferred_element_type=jnp.float32
        ).reshape(values_full.shape)
        return assemble_local(cell_scale[:, None, None] * kinetic + shift * values_full)

    source = adjoint_source.astype(jnp.float32)
    shift = base_potential[:, None, :] - eigenvalues[None, :, None]
    iterate = relax * source
    for step_index in range(ITERS):
        image = operator(iterate.astype(jnp.bfloat16), iterate, shift)
        iterate = iterate + relax * (source - image)
    adjoint = iterate.astype(jnp.bfloat16)
    partial_density = jnp.sum(orbitals.astype(jnp.float32) * iterate, axis=1)
    restrict_full = restrict.astype(jnp.float32)
    density_term = lax.psum(partial_density, "orb")
    projected = jnp.dot(density_term, restrict_full, precision=lax.Precision.HIGHEST)
    coarse_cols = projected.shape[1]
    dest_owner = owner[:, 0]
    owner_hot = (dest_owner[:, None] == jnp.arange(n_domains, dtype=jnp.int32)[None, :]).astype(
        jnp.int32
    )
    earlier = jnp.cumsum(owner_hot, axis=0) - owner_hot
    rank_within = jnp.sum(earlier * owner_hot, axis=1)
    slot_index = dest_owner * capacity + rank_within
    send_hot_int = (
        slot_index[None, :] == jnp.arange(n_domains * capacity, dtype=jnp.int32)[:, None]
    ).astype(jnp.int32)
    send_hot = send_hot_int.astype(jnp.float32)
    send_values = jnp.dot(send_hot, projected, precision=lax.Precision.HIGHEST).reshape(
        n_domains, capacity, coarse_cols
    )
    send_ids = (jnp.sum(send_hot_int * (pot_slot + 1)[None, :], axis=1) - 1).reshape(
        n_domains, capacity
    )
    recv_values, recv_ids = (
        lax.all_to_all(send_values, "dom", split_axis=0, concat_axis=0, tiled=True),
        lax.all_to_all(send_ids, "dom", split_axis=0, concat_axis=0, tiled=True),
    )
    recv_hot = (
        recv_ids.reshape(-1)[None, :] == jnp.arange(pot_rows, dtype=jnp.int32)[:, None]
    ).astype(jnp.float32)
    summed = jnp.dot(
        recv_hot, recv_values.reshape(-1, coarse_cols), precision=lax.Precision.HIGHEST
    )
    updated = potential - step_rate * summed
    every_pot = lax.all_gather(updated, "dom", axis=0, tiled=True)
    cell_pot = every_pot[dest_owner * pot_rows + pot_slot]
    node_potential = jnp.dot(cell_pot, prolong.astype(jnp.float32), precision=lax.Precision.HIGHEST)
    shift_new = (base_potential + node_potential)[:, None, :]
    applied = operator(orbitals, orbitals.astype(jnp.float32), shift_new).astype(jnp.bfloat16)
    return (adjoint, updated, applied)


def solution(mesh):
    in_specs = (
        P("dom", "orb", None),
        P("dom", "orb", None),
        P("orb"),
        P("dom"),
        P("dom", None),
        P(),
        P("dom", None),
        P(),
        P(),
        P("dom", None),
        P("dom"),
        P("dom", None),
    )
    out_specs = (P("dom", "orb", None), P("dom", None), P("dom", "orb", None))
    return jax.shard_map(local, mesh=mesh, in_specs=in_specs, out_specs=out_specs, check_vma=False)
```

profile of v0, /device:TPU:2, one launch (start us, length us, event | category | flops | bytes accessed | tf_op | source)
XLA Modules:
  0.0 320.8 jit_solution(6365384118985894531)
XLA Ops:
  7.2 0.0 all-reduce.2.cloned.1.call-start
  7.3 1.0 copy-done
  8.2 1.6 fusion.10
  9.8 11.4 %collective-permute-start.1 = (f32[1,8,64]{2,1,0:T(8,128)S(1)}, f32[1,8,64]{2,1,0:T(8,128)S(1)}, u32[]{:S(2)}, u32[]{:S(2)}) collective-permute-start(f32[1,8,64]{2,1,0:T(8,128)S(1)} %slice.159), channel_id=1, source_target_pairs={{8,0},{16,8},{24,16},{32,24},{40,32},{48,40},{56,48},{64,56},{72,6... | collective-permute-start | bytes 6152 | tf_op jit(solution)/shard_map/ppermute | solution.py:19
  21.2 1.4 fusion.9
  22.7 1.9 collective-permute-start
  24.6 0.1 fusion.77
  24.7 0.1 reduce_window_sum.11
  24.7 0.2 select_reduce_fusion.1
  24.9 0.1 select_reduce_fusion
  25.1 0.2 slice.157
  25.4 1.4 fusion.15
  26.8 3.5 %collective-permute-done = f32[1,8,64]{2,1,0:T(8,128)S(1)} collective-permute-done((f32[1,8,64]{2,1,0:T(8,128)S(1)}, f32[1,8,64]{2,1,0:T(8,128)S(1)}, u32[]{:S(2)}, u32[]{:S(2)}) %collective-permute-start) | collective-permute-done | bytes 2080 | tf_op jit(solution)/shard_map/ppermute | solution.py:16
  30.3 0.8 fusion.11
  31.2 2.6 collective-permute-start.3
  33.8 1.4 fusion.7
  35.3 0.2 slice.164
  35.5 3.3 %collective-permute-start.2 = (f32[1,8,64]{2,1,0:T(8,128)S(1)}, f32[1,8,64]{2,1,0:T(8,128)S(1)}, u32[]{:S(2)}, u32[]{:S(2)}) collective-permute-start(f32[1,8,64]{2,1,0:T(8,128)S(1)} %slice.162), channel_id=1, source_target_pairs={{0,8},{8,16},{16,24},{24,32},{32,40},{40,48},{48,56},{56,64},{64,7... | collective-permute-start | bytes 6152 | tf_op jit(solution)/shard_map/ppermute | solution.py:16
  38.8 1.4 fusion.16
  40.2 2.9 collective-permute-done.2
  43.2 0.6 fusion.27
  43.8 0.4 fusion.12
  44.2 1.9 collective-permute-start.5
  46.1 1.4 fusion.5
  47.6 0.2 slice.171
  47.8 3.9 %collective-permute-start.4 = (f32[1,8,64]{2,1,0:T(8,128)S(1)}, f32[1,8,64]{2,1,0:T(8,128)S(1)}, u32[]{:S(2)}, u32[]{:S(2)}) collective-permute-start(f32[1,8,64]{2,1,0:T(8,128)S(1)} %slice.169), channel_id=1, source_target_pairs={{0,8},{8,16},{16,24},{24,32},{32,40},{40,48},{48,56},{56,64},{64,7... | collective-permute-start | bytes 6152 | tf_op jit(solution)/shard_map/ppermute | solution.py:16
  51.8 1.4 fusion.17
  53.2 2.3 collective-permute-done.4
  55.5 0.8 fusion.13
  56.3 1.9 collective-permute-start.7
  58.3 1.4 fusion.3
  59.8 0.2 slice.178
  60.0 3.9 %collective-permute-start.6 = (f32[1,8,64]{2,1,0:T(8,128)S(1)}, f32[1,8,64]{2,1,0:T(8,128)S(1)}, u32[]{:S(2)}, u32[]{:S(2)}) collective-permute-start(f32[1,8,64]{2,1,0:T(8,128)S(1)} %slice.176), channel_id=1, source_target_pairs={{0,8},{8,16},{16,24},{24,32},{32,40},{40,48},{48,56},{56,64},{64,7... | collective-permute-start | bytes 6152 | tf_op jit(solution)/shard_map/ppermute | solution.py:16
  63.9 1.4 fusion.18
  65.3 2.3 collective-permute-done.6
  67.7 2.1 fusion.24
  69.8 0.0 all-reduce.2.cloned.1.call-update
  69.8 0.8 sub.46
  70.5 5.7 %all-to-all-start = ((s32[64,1,2]{2,1,0:T(1,128)}), s32[64,1,2]{2,1,0:T(1,128)S(1)}, u32[]{:S(2)}, u32[]{:S(2)}) async-start(s32[64,1,2]{2,1,0:T(1,128)} %bitcast.2), calls=%async_computation | async-start | bytes 65536 | tf_op jit(solution)/shard_map/all_to_all | solution.py:103
  76.3 58.1 %all-reduce.2.cloned.1.call-done = f32[48,512]{1,0:T(8,128)} async-done(((f32[48,512]{1,0:T(8,128)}), f32[48,512]{1,0:T(8,128)}) %all-reduce.2.cloned.1.call-update) | async-done | bytes 98320 | tf_op jit(solution)/shard_map/psum | solution.py:81
  134.3 1.1 fusion.90
  135.4 0.3 fusion.74
  135.8 0.7 reshape.85
  136.5 15.9 %all-to-all-start.1 = ((f32[64,1,128]{2,1,0:T(1,128)}), f32[64,1,128]{2,1,0:T(1,128)S(1)}, u32[]{:S(2)}, u32[]{:S(2)}) async-start(f32[64,1,128]{2,1,0:T(1,128)} %reshape.85), calls=%async_computation.1 | async-start | bytes 65536 | tf_op jit(solution)/shard_map/all_to_all | solution.py:102
  152.4 0.0 all-gather.2.cloned.1.call-start
  152.5 0.5 broadcast.70
  153.0 0.7 reduce.3
  153.7 0.1 eq.63
  153.8 12.0 %all-to-all-done.1 = f32[64,1,128]{2,1,0:T(1,128)S(1)} async-done(((f32[64,1,128]{2,1,0:T(1,128)}), f32[64,1,128]{2,1,0:T(1,128)S(1)}, u32[]{:S(2)}, u32[]{:S(2)}) %all-to-all-start.1) | async-done | bytes 32800 | tf_op jit(solution)/shard_map/all_to_all | solution.py:102
  165.9 0.5 broadcast.72
  166.4 0.7 reduce.4
  167.1 0.1 reshape.86
  167.2 0.8 fusion.21
  168.0 128.1 %all-gather.2.cloned.1.call-done = f32[4096,64]{1,0:T(8,128)} async-done(((f32[64,64]{1,0:T(8,128)}), f32[4096,64]{1,0:T(8,128)}) %all-gather.2.cloned.1.call-update) | async-done | bytes 1048592 | tf_op jit(solution)/shard_map/all_gather | solution.py:112
  296.1 2.2 gather_fusion
  298.3 0.2 convolution_add_fusion
  298.5 0.4 fusion.14
  298.9 4.8 %collective-permute-start.9 = (f32[1,8,64]{2,1,0:T(8,128)S(1)}, f32[1,8,64]{2,1,0:T(8,128)S(1)}, u32[]{:S(2)}, u32[]{:S(2)}) collective-permute-start(f32[1,8,64]{2,1,0:T(8,128)S(1)} %slice.187), channel_id=1, source_target_pairs={{8,0},{16,8},{24,16},{32,24},{40,32},{48,40},{56,48},{64,56},{72,6... | collective-permute-start | bytes 6152 | tf_op jit(solution)/shard_map/ppermute | solution.py:19
  303.7 1.4 fusion.1
  305.2 0.1 slice.211
  305.4 1.9 collective-permute-start.8
  307.3 1.6 fusion.20
  308.9 4.1 %collective-permute-done.8 = f32[1,8,64]{2,1,0:T(8,128)S(1)} collective-permute-done((f32[1,8,64]{2,1,0:T(8,128)S(1)}, f32[1,8,64]{2,1,0:T(8,128)S(1)}, u32[]{:S(2)}, u32[]{:S(2)}) %collective-permute-start.8) | collective-permute-done | bytes 2080 | tf_op jit(solution)/shard_map/ppermute | solution.py:16
  313.0 1.0 pad_maximum_fusion
  (58 shorter events, 0.6 us)
Async XLA Ops:
  7.2 1.0 copy-start
  7.2 14.0 %copy-start.11 = (s32[48,64]{1,0:T(8,128)S(1)}, s32[48,64]{1,0:T(8,128)}, u32[]{:S(2)}) copy-start(s32[48,64]{1,0:T(8,128)} %param.18) | copy-start | bytes 36868
  7.2 17.4 %copy-start.7 = (s32[48,1]{0,1:T(1,128)S(1)}, s32[48,1]{0,1:T(1,128)}, u32[]{:S(2)}) copy-start(s32[48,1]{0,1:T(1,128)} %param.21) | copy-start | bytes 580
  7.2 17.7 %copy-start.9 = (s32[48]{0:T(128)S(1)}, s32[48]{0:T(128)}, u32[]{:S(2)}) copy-start(s32[48]{0:T(128)} %param.22) | copy-start | bytes 580
  7.2 127.1 %all-reduce.2.cloned.1.call-start = ((), (), s32[]{:S(2)}) async-start(), calls=%async_computation.2 | async-start | bytes 196608 | tf_op jit(solution)/shard_map/psum | solution.py:81
  9.8 15.5 %collective-permute-start.1 = (f32[1,8,64]{2,1,0:T(8,128)S(1)}, f32[1,8,64]{2,1,0:T(8,128)S(1)}, u32[]{:S(2)}, u32[]{:S(2)}) collective-permute-start(f32[1,8,64]{2,1,0:T(8,128)S(1)} %slice.159), channel_id=1, source_target_pairs={{8,0},{16,8},{24,16},{32,24},{40,32},{48,40},{56,48},{64,56},{72,6... | collective-permute-start | bytes 6152 | tf_op jit(solution)/shard_map/ppermute | solution.py:19
  22.7 7.6 %collective-permute-start = (f32[1,8,64]{2,1,0:T(8,128)S(1)}, f32[1,8,64]{2,1,0:T(8,128)S(1)}, u32[]{:S(2)}, u32[]{:S(2)}) collective-permute-start(f32[1,8,64]{2,1,0:T(8,128)S(1)} %slice.155), channel_id=1, source_target_pairs={{0,8},{8,16},{16,24},{24,32},{32,40},{40,48},{48,56},{56,64},{64,7... | collective-permute-start | bytes 6152 | tf_op jit(solution)/shard_map/ppermute | solution.py:16
  25.0 5.3 %copy-start.1 = (bf16[48,8,512]{2,1,0:T(8,128)(2,1)S(1)}, bf16[48,8,512]{2,1,0:T(8,128)(2,1)}, u32[]{:S(2)}) copy-start(bf16[48,8,512]{2,1,0:T(8,128)(2,1)} %param.13) | copy-start | bytes 1179652
  25.1 5.3 %copy-start.3 = (f32[48,512]{1,0:T(8,128)S(1)}, f32[48,512]{1,0:T(8,128)}, u32[]{:S(2)}) copy-start(f32[48,512]{1,0:T(8,128)} %param.16) | copy-start | bytes 294916
  25.1 5.3 %copy-start.8 = (f32[48]{0:T(128)S(1)}, f32[48]{0:T(128)}, u32[]{:S(2)}) copy-start(f32[48]{0:T(128)} %param.15) | copy-start | bytes 580
  25.1 5.3 %copy-start.10 = (f32[8]{0:T(128)S(1)}, f32[8]{0:T(128)}, u32[]{:S(2)}) copy-start(f32[8]{0:T(128)} %param.14) | copy-start | bytes 100
  31.2 7.6 %collective-permute-start.3 = (f32[1,8,64]{2,1,0:T(8,128)S(1)}, f32[1,8,64]{2,1,0:T(8,128)S(1)}, u32[]{:S(2)}, u32[]{:S(2)}) collective-permute-start(f32[1,8,64]{2,1,0:T(8,128)S(1)} %slice.166), channel_id=1, source_target_pairs={{8,0},{16,8},{24,16},{32,24},{40,32},{48,40},{56,48},{64,56},{72,6... | collective-permute-start | bytes 6152 | tf_op jit(solution)/shard_map/ppermute | solution.py:19
  35.5 7.6 %collective-permute-start.2 = (f32[1,8,64]{2,1,0:T(8,128)S(1)}, f32[1,8,64]{2,1,0:T(8,128)S(1)}, u32[]{:S(2)}, u32[]{:S(2)}) collective-permute-start(f32[1,8,64]{2,1,0:T(8,128)S(1)} %slice.162), channel_id=1, source_target_pairs={{0,8},{8,16},{16,24},{24,32},{32,40},{40,48},{48,56},{56,64},{64,7... | collective-permute-start | bytes 6152 | tf_op jit(solution)/shard_map/ppermute | solution.py:16
  44.2 7.6 %collective-permute-start.5 = (f32[1,8,64]{2,1,0:T(8,128)S(1)}, f32[1,8,64]{2,1,0:T(8,128)S(1)}, u32[]{:S(2)}, u32[]{:S(2)}) collective-permute-start(f32[1,8,64]{2,1,0:T(8,128)S(1)} %slice.173), channel_id=1, source_target_pairs={{8,0},{16,8},{24,16},{32,24},{40,32},{48,40},{56,48},{64,56},{72,6... | collective-permute-start | bytes 6152 | tf_op jit(solution)/shard_map/ppermute | solution.py:19
  47.8 7.6 %collective-permute-start.4 = (f32[1,8,64]{2,1,0:T(8,128)S(1)}, f32[1,8,64]{2,1,0:T(8,128)S(1)}, u32[]{:S(2)}, u32[]{:S(2)}) collective-permute-start(f32[1,8,64]{2,1,0:T(8,128)S(1)} %slice.169), channel_id=1, source_target_pairs={{0,8},{8,16},{16,24},{24,32},{32,40},{40,48},{48,56},{56,64},{64,7... | collective-permute-start | bytes 6152 | tf_op jit(solution)/shard_map/ppermute | solution.py:16
  56.3 7.6 %collective-permute-start.7 = (f32[1,8,64]{2,1,0:T(8,128)S(1)}, f32[1,8,64]{2,1,0:T(8,128)S(1)}, u32[]{:S(2)}, u32[]{:S(2)}) collective-permute-start(f32[1,8,64]{2,1,0:T(8,128)S(1)} %slice.180), channel_id=1, source_target_pairs={{8,0},{16,8},{24,16},{32,24},{40,32},{48,40},{56,48},{64,56},{72,6... | collective-permute-start | bytes 6152 | tf_op jit(solution)/shard_map/ppermute | solution.py:19
  59.7 8.0 %copy-start.2 = (bf16[48,8,512]{2,1,0:T(8,128)(2,1)S(1)}, bf16[48,8,512]{2,1,0:T(8,128)(2,1)}, u32[]{:S(2)}) copy-start(bf16[48,8,512]{2,1,0:T(8,128)(2,1)} %param.12) | copy-start | bytes 1179652
  60.0 7.6 %collective-permute-start.6 = (f32[1,8,64]{2,1,0:T(8,128)S(1)}, f32[1,8,64]{2,1,0:T(8,128)S(1)}, u32[]{:S(2)}, u32[]{:S(2)}) collective-permute-start(f32[1,8,64]{2,1,0:T(8,128)S(1)} %slice.176), channel_id=1, source_target_pairs={{0,8},{8,16},{16,24},{24,32},{32,40},{40,48},{48,56},{56,64},{64,7... | collective-permute-start | bytes 6152 | tf_op jit(solution)/shard_map/ppermute | solution.py:16
  67.6 66.7 %copy-start.4 = (bf16[512,64]{0,1:T(8,128)(2,1)S(1)}, bf16[512,64]{0,1:T(8,128)(2,1)}, u32[]{:S(2)}) copy-start(bf16[512,64]{0,1:T(8,128)(2,1)} %param.19) | copy-start | bytes 196612
  67.7 99.5 %copy-start.6 = (f32[64,64]{1,0:T(8,128)S(1)}, f32[64,64]{1,0:T(8,128)}, u32[]{:S(2)}) copy-start(f32[64,64]{1,0:T(8,128)} %param.23) | copy-start | bytes 49156
  67.7 230.6 %copy-start.5 = (bf16[64,512]{1,0:T(8,128)(2,1)S(1)}, bf16[64,512]{1,0:T(8,128)(2,1)}, u32[]{:S(2)}) copy-start(bf16[64,512]{1,0:T(8,128)(2,1)} %param.20) | copy-start | bytes 196612
  70.5 65.9 %all-to-all-start = ((s32[64,1,2]{2,1,0:T(1,128)}), s32[64,1,2]{2,1,0:T(1,128)S(1)}, u32[]{:S(2)}, u32[]{:S(2)}) async-start(s32[64,1,2]{2,1,0:T(1,128)} %bitcast.2), calls=%async_computation | async-start | bytes 65536 | tf_op jit(solution)/shard_map/all_to_all | solution.py:103
  136.5 29.4 %all-to-all-start.1 = ((f32[64,1,128]{2,1,0:T(1,128)}), f32[64,1,128]{2,1,0:T(1,128)S(1)}, u32[]{:S(2)}, u32[]{:S(2)}) async-start(f32[64,1,128]{2,1,0:T(1,128)} %reshape.85), calls=%async_computation.1 | async-start | bytes 65536 | tf_op jit(solution)/shard_map/all_to_all | solution.py:102
  152.4 143.7 %all-gather.2.cloned.1.call-start = ((), (), s32[]{:S(2)}) async-start(), calls=%async_computation.3 | async-start | bytes 2129920 | tf_op jit(solution)/shard_map/all_gather | solution.py:112
  298.9 8.4 %collective-permute-start.9 = (f32[1,8,64]{2,1,0:T(8,128)S(1)}, f32[1,8,64]{2,1,0:T(8,128)S(1)}, u32[]{:S(2)}, u32[]{:S(2)}) collective-permute-start(f32[1,8,64]{2,1,0:T(8,128)S(1)} %slice.187), channel_id=1, source_target_pairs={{8,0},{16,8},{24,16},{32,24},{40,32},{48,40},{56,48},{64,56},{72,6... | collective-permute-start | bytes 6152 | tf_op jit(solution)/shard_map/ppermute | solution.py:19
  305.4 7.6 %collective-permute-start.8 = (f32[1,8,64]{2,1,0:T(8,128)S(1)}, f32[1,8,64]{2,1,0:T(8,128)S(1)}, u32[]{:S(2)}, u32[]{:S(2)}) collective-permute-start(f32[1,8,64]{2,1,0:T(8,128)S(1)} %slice.183), channel_id=1, source_target_pairs={{0,8},{8,16},{16,24},{24,32},{32,40},{40,48},{48,56},{56,64},{64,7... | collective-permute-start | bytes 6152 | tf_op jit(solution)/shard_map/ppermute | solution.py:16
Sparse Core Ops, SparseCore 0:
  69.9 64.3 all-reduce.1
  168.1 127.9 all-gather.1
where the time goes:
time: 321 us
  waiting for transfers between devices  213 us (66%)
  starting transfers between devices  59.2 us (18%)
  matrix products  20.7 us (6%)
  between operations  14.7 us (5%)
  local copies, waits for them, and re-layouts  7.21 us (2%)
  other arithmetic  5.72 us (2%)
    all_gather x1, waiting for transfers between devices, local(): every_pot = lax.all_gather(updated, 'dom', axis=0, tiled=True)  128 us
    psum x1, waiting for transfers between devices, local(): density_term = lax.psum(partial_density, 'orb')  58.1 us
    ppermute x5, starting transfers between devices, padded_2(): lax.ppermute(lax.slice_in_dim(block, 0, width, axis=dim), axis, backward)  22.6 us
    all_to_all x1, starting transfers between devices, local(): lax.all_to_all(send_values, 'dom', split_axis=0, concat_axis=0, tiled=True)  15.9 us
    ppermute x5, waiting for transfers between devices, padded_2(): lax.ppermute(lax.slice_in_dim(block, block.shape[dim] - width, None, axis...  15 us
    ppermute x5, starting transfers between devices, padded_2(): lax.ppermute(lax.slice_in_dim(block, block.shape[dim] - width, None, axis...  15 us
    all_to_all x1, waiting for transfers between devices, local(): lax.all_to_all(send_values, 'dom', split_axis=0, concat_axis=0, tiled=True)  12 us
    dot_general x5, matrix products, assemble_local(): jnp.einsum('ckj,coj->cok', onehot, left_next, precision=lax.Precision.HIG...  7.2 us
  transfers between devices with their start and end apart: 14, of which 8 were waited for; matrix products, arithmetic and copies ran while one was open for 6% of the time, Pallas kernels for 0%

commit v1 on v0

--- a/solution.py
+++ b/solution.py
@@ -78,7 +78,7 @@
     adjoint = iterate.astype(jnp.bfloat16)
     partial_density = jnp.sum(orbitals.astype(jnp.float32) * iterate, axis=1)
     restrict_full = restrict.astype(jnp.float32)
-    density_term = lax.psum(partial_density, "orb")
+    density_term = jnp.sum(lax.all_gather(partial_density, axis_name="orb"), axis=0)
     projected = jnp.dot(density_term, restrict_full, precision=lax.Precision.HIGHEST)
     coarse_cols = projected.shape[1]
     dest_owner = owner[:, 0]

time: 321 us -> 279 us (0.87)
  waiting for transfers between devices: 213 us -> 157 us
  blocking collectives: 0 us -> 14.3 us
    psum x1 -> x0, waiting for transfers between devices: 58.1 us -> none  [local(): density_term = lax.psum(partial_density, 'orb')]
    all_gather x0 -> x1, blocking collectives: none -> 14.3 us  [local(): lax.all_gather(partial_density, axis_name='orb')]
    all_to_all x1, starting transfers between devices: 5.7 us -> 18.6 us  [local(): lax.all_to_all(send_ids, 'dom', split_axis=0, concat_axis=0, tiled=True)]
    ppermute x5, starting transfers between devices: 22.6 us -> 15.3 us  [padded_2(): lax.ppermute(lax.slice_in_dim(block, 0, width, axis=dim), axis, backward)]
    all_to_all x1, starting transfers between devices: 15.9 us -> 9.42 us  [local(): lax.all_to_all(send_values, 'dom', split_axis=0, concat_axis=0, tiled=True)]
  transfers between devices with their start and end apart: 14 -> 13, of which waited for: 8 -> 7; matrix products, arithmetic and copies ran while one was open for 6% -> 9% of each run, Pallas kernels for 0% -> 0%
where the time goes in v1:
time: 279 us; the launch traced here: 278 us
  waiting for transfers between devices  157 us (56%)
  starting transfers between devices  59 us (21%)
  matrix products  19.8 us (7%)
  between operations  14.6 us (5%)
  blocking collectives  14.3 us (5%)
  other arithmetic  7.18 us (3%)
  local copies, waits for them, and re-layouts  6.25 us (2%)
    all_gather x1, waiting for transfers between devices, local(): every_pot = lax.all_gather(updated, 'dom', axis=0, tiled=True)  130 us
    all_to_all x1, starting transfers between devices, local(): lax.all_to_all(send_ids, 'dom', split_axis=0, concat_axis=0, tiled=True)  18.6 us
    ppermute x5, starting transfers between devices, padded_2(): lax.ppermute(lax.slice_in_dim(block, block.shape[dim] - width, None, axis...  15.6 us
    ppermute x5, starting transfers between devices, padded_2(): lax.ppermute(lax.slice_in_dim(block, 0, width, axis=dim), axis, backward)  15.3 us
    ppermute x5, waiting for transfers between devices, padded_2(): lax.ppermute(lax.slice_in_dim(block, block.shape[dim] - width, None, axis...  15 us
    all_gather x1, blocking collectives, local(): lax.all_gather(partial_density, axis_name='orb')  14.3 us
    all_to_all x1, waiting for transfers between devices, local(): lax.all_to_all(send_values, 'dom', split_axis=0, concat_axis=0, tiled=True)  12 us
    all_to_all x1, starting transfers between devices, local(): lax.all_to_all(send_values, 'dom', split_axis=0, concat_axis=0, tiled=True)  9.42 us
  transfers between devices with their start and end apart: 13, of which 7 were waited for; matrix products, arithmetic and copies ran while one was open for 9% of the time, Pallas kernels for 0%

profile of v1, /device:TPU:2, one launch (start us, length us, event | category | flops | bytes accessed | tf_op | source)
XLA Modules:
  0.0 278.3 jit_solution(2145143908049543588)
XLA Ops:
  7.2 0.8 fusion.77
  8.0 0.1 reduce_window_sum.11
  8.0 0.8 select_reduce_fusion.1
  8.9 0.7 compare_select_fusion
  9.6 0.1 select_reduce_fusion
  9.7 0.8 sub.46
  10.4 18.6 %all-to-all-start = ((s32[64,1,2]{2,1,0:T(1,128)}), s32[64,1,2]{2,1,0:T(1,128)S(1)}, u32[]{:S(2)}, u32[]{:S(2)}) async-start(s32[64,1,2]{2,1,0:T(1,128)} %bitcast.2), calls=%async_computation | async-start | bytes 65536 | tf_op jit(solution)/shard_map/all_to_all | solution.py:103
  29.1 1.6 fusion.10
  30.7 4.6 %collective-permute-start.1 = (f32[1,8,64]{2,1,0:T(8,128)S(1)}, f32[1,8,64]{2,1,0:T(8,128)S(1)}, u32[]{:S(2)}, u32[]{:S(2)}) collective-permute-start(f32[1,8,64]{2,1,0:T(8,128)S(1)} %slice.159), channel_id=1, source_target_pairs={{8,0},{16,8},{24,16},{32,24},{40,32},{48,40},{56,48},{64,56},{72,6... | collective-permute-start | bytes 6152 | tf_op jit(solution)/shard_map/ppermute | solution.py:19
  35.3 1.4 fusion.9
  36.8 2.1 collective-permute-start
  38.9 0.2 slice.157
  39.1 1.4 fusion.15
  40.5 4.0 %collective-permute-done = f32[1,8,64]{2,1,0:T(8,128)S(1)} collective-permute-done((f32[1,8,64]{2,1,0:T(8,128)S(1)}, f32[1,8,64]{2,1,0:T(8,128)S(1)}, u32[]{:S(2)}, u32[]{:S(2)}) %collective-permute-start) | collective-permute-done | bytes 2080 | tf_op jit(solution)/shard_map/ppermute | solution.py:16
  44.6 0.8 fusion.11
  45.5 2.1 collective-permute-start.3
  47.5 1.4 fusion.7
  49.0 0.2 slice.164
  49.3 3.8 %collective-permute-start.2 = (f32[1,8,64]{2,1,0:T(8,128)S(1)}, f32[1,8,64]{2,1,0:T(8,128)S(1)}, u32[]{:S(2)}, u32[]{:S(2)}) collective-permute-start(f32[1,8,64]{2,1,0:T(8,128)S(1)} %slice.162), channel_id=1, source_target_pairs={{0,8},{8,16},{16,24},{24,32},{32,40},{40,48},{48,56},{56,64},{64,7... | collective-permute-start | bytes 6152 | tf_op jit(solution)/shard_map/ppermute | solution.py:16
  53.1 1.4 fusion.16
  54.5 2.4 collective-permute-done.2
  56.9 0.6 fusion.27
  57.5 0.4 fusion.12
  57.9 1.9 collective-permute-start.5
  59.9 1.4 fusion.5
  61.4 0.2 slice.171
  61.6 3.9 %collective-permute-start.4 = (f32[1,8,64]{2,1,0:T(8,128)S(1)}, f32[1,8,64]{2,1,0:T(8,128)S(1)}, u32[]{:S(2)}, u32[]{:S(2)}) collective-permute-start(f32[1,8,64]{2,1,0:T(8,128)S(1)} %slice.169), channel_id=1, source_target_pairs={{0,8},{8,16},{16,24},{24,32},{32,40},{40,48},{48,56},{56,64},{64,7... | collective-permute-start | bytes 6152 | tf_op jit(solution)/shard_map/ppermute | solution.py:16
  65.5 1.4 fusion.17
  66.9 2.3 collective-permute-done.4
  69.2 0.8 fusion.13
  70.1 1.9 collective-permute-start.7
  72.0 1.4 fusion.3
  73.5 0.2 slice.178
  73.7 3.9 %collective-permute-start.6 = (f32[1,8,64]{2,1,0:T(8,128)S(1)}, f32[1,8,64]{2,1,0:T(8,128)S(1)}, u32[]{:S(2)}, u32[]{:S(2)}) collective-permute-start(f32[1,8,64]{2,1,0:T(8,128)S(1)} %slice.176), channel_id=1, source_target_pairs={{0,8},{8,16},{16,24},{24,32},{32,40},{40,48},{48,56},{56,64},{64,7... | collective-permute-start | bytes 6152 | tf_op jit(solution)/shard_map/ppermute | solution.py:16
  77.7 1.4 fusion.18
  79.1 2.3 collective-permute-done.6
  81.4 1.4 fusion.24
  82.8 14.3 %all-gather = f32[384,512]{1,0:T(8,128)S(1)} all-gather(f32[48,512]{1,0:T(8,128)S(1)} %get-tuple-element.3), channel_id=2, replica_groups=mesh['dom'=64,'orb'=8] {'orb'}, dimensions={0}, use_global_device_ids=true | all-gather | bytes 884736 | tf_op jit(solution)/shard_map/all_gather | solution.py:81
  97.1 0.1 reduce_sum.39
  97.2 0.2 fusion.90
  97.4 0.3 fusion.74
  97.7 0.7 reshape.86
  98.5 9.4 %all-to-all-start.1 = ((f32[64,1,128]{2,1,0:T(1,128)}), f32[64,1,128]{2,1,0:T(1,128)S(1)}, u32[]{:S(2)}, u32[]{:S(2)}) async-start(f32[64,1,128]{2,1,0:T(1,128)} %reshape.86), calls=%async_computation.1 | async-start | bytes 65536 | tf_op jit(solution)/shard_map/all_to_all | solution.py:102
  107.9 0.0 all-gather.3.cloned.1.call-start
  107.9 0.5 broadcast.70
  108.5 0.7 reduce.3
  109.2 0.1 eq.63
  109.3 12.0 %all-to-all-done.1 = f32[64,1,128]{2,1,0:T(1,128)S(1)} async-done(((f32[64,1,128]{2,1,0:T(1,128)}), f32[64,1,128]{2,1,0:T(1,128)S(1)}, u32[]{:S(2)}, u32[]{:S(2)}) %all-to-all-start.1) | async-done | bytes 32800 | tf_op jit(solution)/shard_map/all_to_all | solution.py:102
  121.3 0.5 broadcast.72
  121.9 0.7 reduce.4
  122.6 0.1 reshape.87
  122.7 0.8 fusion.21
  123.5 0.0 all-gather.3.cloned.1.call-update
  123.5 130.0 %all-gather.3.cloned.1.call-done = f32[4096,64]{1,0:T(8,128)} async-done(((f32[64,64]{1,0:T(8,128)}), f32[4096,64]{1,0:T(8,128)}) %all-gather.3.cloned.1.call-update) | async-done | bytes 1048592 | tf_op jit(solution)/shard_map/all_gather | solution.py:112
  253.5 2.2 gather_fusion
  255.7 0.2 convolution_add_fusion
  255.9 0.4 fusion.14
  256.3 4.8 %collective-permute-start.9 = (f32[1,8,64]{2,1,0:T(8,128)S(1)}, f32[1,8,64]{2,1,0:T(8,128)S(1)}, u32[]{:S(2)}, u32[]{:S(2)}) collective-permute-start(f32[1,8,64]{2,1,0:T(8,128)S(1)} %slice.187), channel_id=1, source_target_pairs={{8,0},{16,8},{24,16},{32,24},{40,32},{48,40},{56,48},{64,56},{72,6... | collective-permute-start | bytes 6152 | tf_op jit(solution)/shard_map/ppermute | solution.py:19
  261.1 1.4 fusion.1
  262.6 0.1 slice.211
  262.8 1.9 collective-permute-start.8
  264.7 1.6 fusion.20
  266.3 4.1 %collective-permute-done.8 = f32[1,8,64]{2,1,0:T(8,128)S(1)} collective-permute-done((f32[1,8,64]{2,1,0:T(8,128)S(1)}, f32[1,8,64]{2,1,0:T(8,128)S(1)}, u32[]{:S(2)}, u32[]{:S(2)}) %collective-permute-start.8) | collective-permute-done | bytes 2080 | tf_op jit(solution)/shard_map/ppermute | solution.py:16
  270.4 1.0 pad_maximum_fusion
  (53 shorter events, 0.5 us)
Async XLA Ops:
  7.2 21.9 %copy-start = (bf16[512,512]{1,0:T(8,128)(2,1)S(1)}, bf16[512,512]{1,0:T(8,128)(2,1)}, u32[]{:S(2)}) copy-start(bf16[512,512]{1,0:T(8,128)(2,1)} %param.17) | copy-start | bytes 1572868
  7.2 28.1 %copy-start.9 = (s32[48,64]{1,0:T(8,128)S(1)}, s32[48,64]{1,0:T(8,128)}, u32[]{:S(2)}) copy-start(s32[48,64]{1,0:T(8,128)} %param.18) | copy-start | bytes 36868
  10.4 88.0 %all-to-all-start = ((s32[64,1,2]{2,1,0:T(1,128)}), s32[64,1,2]{2,1,0:T(1,128)S(1)}, u32[]{:S(2)}, u32[]{:S(2)}) async-start(s32[64,1,2]{2,1,0:T(1,128)} %bitcast.2), calls=%async_computation | async-start | bytes 65536 | tf_op jit(solution)/shard_map/all_to_all | solution.py:103
  30.7 8.4 %collective-permute-start.1 = (f32[1,8,64]{2,1,0:T(8,128)S(1)}, f32[1,8,64]{2,1,0:T(8,128)S(1)}, u32[]{:S(2)}, u32[]{:S(2)}) collective-permute-start(f32[1,8,64]{2,1,0:T(8,128)S(1)} %slice.159), channel_id=1, source_target_pairs={{8,0},{16,8},{24,16},{32,24},{40,32},{48,40},{56,48},{64,56},{72,6... | collective-permute-start | bytes 6152 | tf_op jit(solution)/shard_map/ppermute | solution.py:19
  36.7 7.8 %copy-start.1 = (bf16[48,8,512]{2,1,0:T(8,128)(2,1)S(1)}, bf16[48,8,512]{2,1,0:T(8,128)(2,1)}, u32[]{:S(2)}) copy-start(bf16[48,8,512]{2,1,0:T(8,128)(2,1)} %param.13) | copy-start | bytes 1179652
  36.8 7.8 %copy-start.3 = (f32[48,512]{1,0:T(8,128)S(1)}, f32[48,512]{1,0:T(8,128)}, u32[]{:S(2)}) copy-start(f32[48,512]{1,0:T(8,128)} %param.16) | copy-start | bytes 294916
  36.8 7.8 %copy-start.7 = (f32[48]{0:T(128)S(1)}, f32[48]{0:T(128)}, u32[]{:S(2)}) copy-start(f32[48]{0:T(128)} %param.15) | copy-start | bytes 580
  36.8 7.8 %copy-start.8 = (f32[8]{0:T(128)S(1)}, f32[8]{0:T(128)}, u32[]{:S(2)}) copy-start(f32[8]{0:T(128)} %param.14) | copy-start | bytes 100
  36.8 7.7 %collective-permute-start = (f32[1,8,64]{2,1,0:T(8,128)S(1)}, f32[1,8,64]{2,1,0:T(8,128)S(1)}, u32[]{:S(2)}, u32[]{:S(2)}) collective-permute-start(f32[1,8,64]{2,1,0:T(8,128)S(1)} %slice.155), channel_id=1, source_target_pairs={{0,8},{8,16},{16,24},{24,32},{32,40},{40,48},{48,56},{56,64},{64,7... | collective-permute-start | bytes 6152 | tf_op jit(solution)/shard_map/ppermute | solution.py:16
  45.5 7.6 %collective-permute-start.3 = (f32[1,8,64]{2,1,0:T(8,128)S(1)}, f32[1,8,64]{2,1,0:T(8,128)S(1)}, u32[]{:S(2)}, u32[]{:S(2)}) collective-permute-start(f32[1,8,64]{2,1,0:T(8,128)S(1)} %slice.166), channel_id=1, source_target_pairs={{8,0},{16,8},{24,16},{32,24},{40,32},{48,40},{56,48},{64,56},{72,6... | collective-permute-start | bytes 6152 | tf_op jit(solution)/shard_map/ppermute | solution.py:19
  49.3 7.6 %collective-permute-start.2 = (f32[1,8,64]{2,1,0:T(8,128)S(1)}, f32[1,8,64]{2,1,0:T(8,128)S(1)}, u32[]{:S(2)}, u32[]{:S(2)}) collective-permute-start(f32[1,8,64]{2,1,0:T(8,128)S(1)} %slice.162), channel_id=1, source_target_pairs={{0,8},{8,16},{16,24},{24,32},{32,40},{40,48},{48,56},{56,64},{64,7... | collective-permute-start | bytes 6152 | tf_op jit(solution)/shard_map/ppermute | solution.py:16
  57.9 7.6 %collective-permute-start.5 = (f32[1,8,64]{2,1,0:T(8,128)S(1)}, f32[1,8,64]{2,1,0:T(8,128)S(1)}, u32[]{:S(2)}, u32[]{:S(2)}) collective-permute-start(f32[1,8,64]{2,1,0:T(8,128)S(1)} %slice.173), channel_id=1, source_target_pairs={{8,0},{16,8},{24,16},{32,24},{40,32},{48,40},{56,48},{64,56},{72,6... | collective-permute-start | bytes 6152 | tf_op jit(solution)/shard_map/ppermute | solution.py:19
  61.6 7.6 %collective-permute-start.4 = (f32[1,8,64]{2,1,0:T(8,128)S(1)}, f32[1,8,64]{2,1,0:T(8,128)S(1)}, u32[]{:S(2)}, u32[]{:S(2)}) collective-permute-start(f32[1,8,64]{2,1,0:T(8,128)S(1)} %slice.169), channel_id=1, source_target_pairs={{0,8},{8,16},{16,24},{24,32},{32,40},{40,48},{48,56},{56,64},{64,7... | collective-permute-start | bytes 6152 | tf_op jit(solution)/shard_map/ppermute | solution.py:16
  70.1 7.6 %collective-permute-start.7 = (f32[1,8,64]{2,1,0:T(8,128)S(1)}, f32[1,8,64]{2,1,0:T(8,128)S(1)}, u32[]{:S(2)}, u32[]{:S(2)}) collective-permute-start(f32[1,8,64]{2,1,0:T(8,128)S(1)} %slice.180), channel_id=1, source_target_pairs={{8,0},{16,8},{24,16},{32,24},{40,32},{48,40},{56,48},{64,56},{72,6... | collective-permute-start | bytes 6152 | tf_op jit(solution)/shard_map/ppermute | solution.py:19
  73.4 8.0 %copy-start.2 = (bf16[48,8,512]{2,1,0:T(8,128)(2,1)S(1)}, bf16[48,8,512]{2,1,0:T(8,128)(2,1)}, u32[]{:S(2)}) copy-start(bf16[48,8,512]{2,1,0:T(8,128)(2,1)} %param.12) | copy-start | bytes 1179652
  73.7 7.6 %collective-permute-start.6 = (f32[1,8,64]{2,1,0:T(8,128)S(1)}, f32[1,8,64]{2,1,0:T(8,128)S(1)}, u32[]{:S(2)}, u32[]{:S(2)}) collective-permute-start(f32[1,8,64]{2,1,0:T(8,128)S(1)} %slice.176), channel_id=1, source_target_pairs={{0,8},{8,16},{16,24},{24,32},{32,40},{40,48},{48,56},{56,64},{64,7... | collective-permute-start | bytes 6152 | tf_op jit(solution)/shard_map/ppermute | solution.py:16
  82.8 14.4 %copy-start.4 = (bf16[512,64]{0,1:T(8,128)(2,1)S(1)}, bf16[512,64]{0,1:T(8,128)(2,1)}, u32[]{:S(2)}) copy-start(bf16[512,64]{0,1:T(8,128)(2,1)} %param.19) | copy-start | bytes 196612
  82.8 39.8 %copy-start.6 = (f32[64,64]{1,0:T(8,128)S(1)}, f32[64,64]{1,0:T(8,128)}, u32[]{:S(2)}) copy-start(f32[64,64]{1,0:T(8,128)} %param.23) | copy-start | bytes 49156
  82.8 172.9 %copy-start.5 = (bf16[64,512]{1,0:T(8,128)(2,1)S(1)}, bf16[64,512]{1,0:T(8,128)(2,1)}, u32[]{:S(2)}) copy-start(bf16[64,512]{1,0:T(8,128)(2,1)} %param.20) | copy-start | bytes 196612
  98.5 22.9 %all-to-all-start.1 = ((f32[64,1,128]{2,1,0:T(1,128)}), f32[64,1,128]{2,1,0:T(1,128)S(1)}, u32[]{:S(2)}, u32[]{:S(2)}) async-start(f32[64,1,128]{2,1,0:T(1,128)} %reshape.86), calls=%async_computation.1 | async-start | bytes 65536 | tf_op jit(solution)/shard_map/all_to_all | solution.py:102
  107.9 145.7 %all-gather.3.cloned.1.call-start = ((), (), s32[]{:S(2)}) async-start(), calls=%async_computation.2 | async-start | bytes 2129920 | tf_op jit(solution)/shard_map/all_gather | solution.py:112
  256.3 8.4 %collective-permute-start.9 = (f32[1,8,64]{2,1,0:T(8,128)S(1)}, f32[1,8,64]{2,1,0:T(8,128)S(1)}, u32[]{:S(2)}, u32[]{:S(2)}) collective-permute-start(f32[1,8,64]{2,1,0:T(8,128)S(1)} %slice.187), channel_id=1, source_target_pairs={{8,0},{16,8},{24,16},{32,24},{40,32},{48,40},{56,48},{64,56},{72,6... | collective-permute-start | bytes 6152 | tf_op jit(solution)/shard_map/ppermute | solution.py:19
  262.8 7.6 %collective-permute-start.8 = (f32[1,8,64]{2,1,0:T(8,128)S(1)}, f32[1,8,64]{2,1,0:T(8,128)S(1)}, u32[]{:S(2)}, u32[]{:S(2)}) collective-permute-start(f32[1,8,64]{2,1,0:T(8,128)S(1)} %slice.183), channel_id=1, source_target_pairs={{0,8},{8,16},{16,24},{24,32},{32,40},{40,48},{48,56},{56,64},{64,7... | collective-permute-start | bytes 6152 | tf_op jit(solution)/shard_map/ppermute | solution.py:16
Sparse Core Ops, SparseCore 0:
  123.6 129.8 all-gather.2
